TPU v7x, 128 devices: a whole 4x4x4 slice. The times are simulated.
128 devices in a mesh: lat: 8 (over x, y_lo), ord: 16 (over y_hi, z, core).
Axes of the slice: x: 4, y: 4 (y_hi: 2, y_lo: 2; y = y_hi * 2 + y_lo), z: 4, core: 2. Of those that a mesh axis runs over, the one named last changes fastest.
Arguments:
- heights: bfloat16 [2048, 43200], P(('lat', 'ord')), may hold values from -1.5 to 1.5
- panels: bfloat16 [2048, 5120, 128], P('lat', 'ord'), may hold values from -0.125 to 0.125
- ord_slot: int32 [5120], replicated, may hold values from 0 to 5119, each once
- cutoffs: int32 [5120], P('ord'), may hold values from 13360 to 21599
Outputs:
- gravity: float32 [2048, 43200], P(('lat', 'ord'))
Inputs may be any that keep to these rules, and one draw needn't show every extreme that they name: `ord_slot`: a permutation of the order slots.
All inputs are finite; a program needn't handle non-finite values.
Results may differ from a plain program's by a relative error of at most 0.0039.
Values may be sent and summed in bfloat16 or wider, within the bound.
A program may use at most 192 MiB of HBM per device.

v0:
```python
import math
import jax
import jax.numpy as jnp
from jax import lax
from jax.sharding import PartitionSpec as P

LON_SLOW = 180
LON_FAST = 240
ORDERS = 5120
DEG = 128
NMAX = 21600


def slow_tables(slow):
    index = jnp.arange(slow, dtype=jnp.int32)
    phase = index[:, None] * index[None, :] % slow
    angle = 2.0 * math.pi / slow * phase.astype(jnp.float32)
    return (jnp.cos(angle), jnp.sin(angle))


def twiddle_tables(slow, fast, blocks):
    total = slow * fast
    first = jnp.arange(slow, dtype=jnp.int32)[:, None, None]
    middle = jnp.arange(fast, dtype=jnp.int32)[None, :, None]
    last = jnp.arange(blocks, dtype=jnp.int32)[None, None, :]
    phase = (middle * first + slow * middle * last) % total
    angle = 2.0 * math.pi / total * phase.astype(jnp.float32)
    return (jnp.cos(angle), jnp.sin(angle))


def forward_spectra(values, slow, fast, orders):
    count = values.shape[0]
    grid = values.reshape(count, slow, fast)
    cosine, sine = slow_tables(slow)
    first_real = jnp.einsum("raj,ak->rkj", grid, cosine, precision=lax.Precision.HIGHEST)
    first_imag = -jnp.einsum("raj,ak->rkj", grid, sine, precision=lax.Precision.HIGHEST)
    blocks = orders // slow + 1
    twist_cos, twist_sin = twiddle_tables(slow, fast, blocks)
    joined = jnp.concatenate([first_real, first_imag], 2)
    table = jnp.concatenate(
        [jnp.concatenate([twist_cos, -twist_sin], 2), jnp.concatenate([twist_sin, twist_cos], 2)], 1
    )
    second = jnp.einsum("rkj,kjq->rkq", joined, table, precision=lax.Precision.HIGHEST)
    scale_in = 1.0 / math.sqrt(slow * fast)
    spec_real = (
        second[:, :, :blocks].transpose(0, 2, 1).reshape(count, blocks * slow)[:, 1 : orders + 1]
    )
    spec_imag = (
        second[:, :, blocks:].transpose(0, 2, 1).reshape(count, blocks * slow)[:, 1 : orders + 1]
    )
    return (spec_real * scale_in, spec_imag * scale_in)


def inverse_field(full_real, full_imag, slow, fast):
    count = full_real.shape[0]
    blocks = full_real.shape[1] // slow
    grid_real = full_real.reshape(count, blocks, slow).transpose(0, 2, 1)
    grid_imag = full_imag.reshape(count, blocks, slow).transpose(0, 2, 1)
    joined = jnp.concatenate([grid_real, grid_imag], 2)
    twist_cos, twist_sin = twiddle_tables(slow, fast, blocks)
    cos_turned = twist_cos.transpose(0, 2, 1)
    sin_turned = twist_sin.transpose(0, 2, 1)
    table = jnp.concatenate(
        [
            jnp.concatenate([cos_turned, sin_turned], 2),
            jnp.concatenate([-sin_turned, cos_turned], 2),
        ],
        1,
    )
    second = jnp.einsum("rkq,kqj->rkj", joined, table, precision=lax.Precision.HIGHEST)
    cosine, sine = slow_tables(slow)
    field = jnp.einsum("rkj,ka->raj", second[:, :, :fast], cosine, precision=lax.Precision.HIGHEST)
    field = field - jnp.einsum(
        "rkj,ka->raj", second[:, :, fast:], sine, precision=lax.Precision.HIGHEST
    )
    return field.reshape(count, slow * fast)


def fold_powers(terms, factors):
    slots = terms.shape[1]
    width = terms.shape[2]
    return jnp.sum(terms.reshape(3, 2, slots, width) * factors[:, None, None, :], axis=0)


def local(heights, panels, ord_slot, cutoffs):
    lat_count = lax.axis_size("lat")
    ord_count = lax.axis_size("ord")
    level = heights.astype(jnp.float32)
    cycle_dev = level.shape[0]
    square = level * level
    powers = jnp.concatenate([level, square, square * level], 0)
    spec_real, spec_imag = forward_spectra(powers, LON_SLOW, LON_FAST, ORDERS)
    picked = jnp.stack(
        [
            spec_real[:, ord_slot].reshape(3, cycle_dev, ORDERS),
            spec_imag[:, ord_slot].reshape(3, cycle_dev, ORDERS),
        ],
        1,
    )
    picked = picked.reshape(6, cycle_dev, ORDERS).astype(jnp.bfloat16)
    sums = jnp.einsum(
        "xrk,rkn->xkn",
        lax.all_to_all(picked, "ord", split_axis=2, concat_axis=1, tiled=True),
        panels,
        preferred_element_type=jnp.float32,
    )
    stride = (NMAX - ORDERS) // DEG
    degree_int = ORDERS + jnp.arange(DEG, dtype=jnp.int32) * stride
    degree = degree_int.astype(jnp.float32)
    factors = jnp.stack(
        [
            jnp.ones_like(degree),
            (degree + 2.0) / (2.0 * NMAX),
            (degree + 2.0) * (degree + 1.0) / (6.0 * NMAX * NMAX),
        ]
    )
    keep = (degree_int[None, :] <= cutoffs[:, None]).astype(jnp.float32)
    total = lax.psum(sums, "lat")
    folded = fold_powers(total, factors)
    coeffs = (folded * keep[None]).astype(jnp.bfloat16)
    synthesis = jnp.einsum("rkn,ckn->crk", panels, coeffs, preferred_element_type=jnp.float32)
    returned = lax.all_to_all(synthesis, "ord", split_axis=1, concat_axis=2, tiled=True)
    blocks = ORDERS // LON_SLOW + 1
    target = ord_slot + 1
    full_real = (
        jnp.zeros((cycle_dev, blocks * LON_SLOW), jnp.float32).at[:, target].set(returned[0])
    )
    full_imag = (
        jnp.zeros((cycle_dev, blocks * LON_SLOW), jnp.float32).at[:, target].set(returned[1])
    )
    field = inverse_field(full_real, full_imag, LON_SLOW, LON_FAST)
    cycles_all = cycle_dev * lat_count * ord_count
    return field * math.sqrt(cycles_all / (DEG * ORDERS))


def solution(mesh):
    return jax.shard_map(
        local,
        mesh=mesh,
        in_specs=(P(("lat", "ord"), None), P("lat", "ord", None), P(), P("ord")),
        out_specs=P(("lat", "ord"), None),
        check_vma=False,
    )
```

profile of v0, /device:TPU:1, one launch (start us, length us, event | category | flops | bytes accessed | tf_op | source)
XLA Modules:
  0.0 490.3 jit_solution(14561908962304863775)
XLA Ops:
  6.5 0.0 all-reduce.2.cloned.1.call-start
  6.5 1.8 convert_multiply_fusion.1
  8.4 0.0 copy-done.1
  8.4 0.2 convert_element_type.66
  8.5 3.5 pad_maximum_fusion.1
  12.1 11.4 %reshape.129 = f32[48,180,240]{2,1,0:T(8,128)} reshape(f32[48,43200]{1,0:T(8,128)} %pad_maximum_fusion.1) | data formatting | bytes 16588800 | tf_op jit(solution)/shard_map/reshape | solution.py:33
  23.5 13.3 %convolution_bitcast_fusion = f32[48,180,240]{2,1,0:T(8,128)S(1)} fusion(f32[48,180,240]{2,1,0:T(8,128)} %reshape.129), kind=kOutput, calls=%fused_computation.48 | convolution fusion | flops 4479267840 | bytes 16588800 | tf_op jit(solution)/shard_map/raj,ak->rkj/dot_general | solution.py:35
  36.8 9.9 %negate_bitcast_fusion = f32[48,180,240]{2,1,0:T(8,128)S(1)} fusion(f32[48,180,240]{2,1,0:T(8,128)S(1)} %copy-done), kind=kOutput, calls=%fused_computation.26 | convolution fusion | flops 4481341440 | bytes 16588800 | tf_op jit(solution)/shard_map/raj,ak->rkj/dot_general | solution.py:36
  46.8 7.9 %pad_maximum_fusion = f32[48,180,480]{2,1,0:T(8,128)} fusion(f32[48,180,240]{2,1,0:T(8,128)S(1)} %negate_bitcast_fusion, f32[48,180,240]{2,1,0:T(8,128)S(1)} %convolution_bitcast_fusion), kind=kLoop, calls=%fused_computation.24 | loop fusion | flops 4147200 | bytes 33177600 | tf_op jit(solution)/shard_map/concatenate | solution.py:39
  54.7 26.4 %fusion.50 = (f32[180,240,29]{1,2,0:T(8,128)}, f32[180,240,29]{1,2,0:T(8,128)}, f32[180,240,29]{1,2,0:T(8,128)}) fusion(s32[240,29]{0,1:T(8,128)S(1)} %iota_multiply_fusion.1, s32[180,240]{1,0:T(8,128)S(1)} %iota_multiply_fusion), kind=kLoop, calls=%fused_computation.59 | loop fusion | flops 12528000 | bytes 15234240 | tf_op jit(solution)/shard_map/neg | solution.py:41
  81.1 38.4 %fusion.42 = f32[48,180,58]{2,0,1:T(8,128)S(1)} fusion(f32[48,180,480]{2,1,0:T(8,128)} %pad_maximum_fusion, f32[180,240,29]{1,2,0:T(8,128)} %get-tuple-element.15, f32[180,240,29]{1,2,0:T(8,128)} %get-tuple-element.14, f32[180,240,29]{1,2,0:T(8,128)} %get-tuple-element.13), kind=kOutput, calls=%fused_computation.57 | convolution fusion | flops 2901484800 | bytes 33626880 | tf_op jit(solution)/shard_map/rkj,kjq->rkq/dot_general | solution.py:43
  119.5 4.8 slice_bitcast_fusion.1
  124.3 4.4 copy.110
  128.7 0.0 copy-start.2
  128.7 1.7 reshape.173
  130.4 2.1 slice_multiply_fusion.1
  132.5 15.1 %gather_fusion = bf16[5120,48]{1,0:T(8,128)(2,1)S(1)} fusion(bf16[48,5120]{0,1:T(8,128)(2,1)S(1)} %slice_multiply_fusion.1, s32[5120]{0:T(1024)S(1)} %get-tuple-element.19), kind=kCustom, calls=%fused_computation | custom fusion | bytes 1003520 | tf_op jit(solution)/shard_map/gather | solution.py:95
  147.6 0.6 copy.85
  148.2 4.4 copy.111
  152.6 1.7 reshape.174
  154.3 2.1 slice_multiply_fusion
  156.4 15.1 %gather_fusion.1 = bf16[5120,48]{1,0:T(8,128)(2,1)S(1)} fusion(bf16[48,5120]{0,1:T(8,128)(2,1)S(1)} %slice_multiply_fusion, s32[5120]{0:T(1024)S(1)} %get-tuple-element.19), kind=kCustom, calls=%fused_computation.1 | custom fusion | bytes 1003520 | tf_op jit(solution)/shard_map/gather | solution.py:96
  171.5 0.6 copy.88
  172.1 0.1 pad_maximum_fusion.2
  172.2 0.1 copy.89
  172.3 8.1 %copy.90 = bf16[6,16,5120]{1,0,2:T(8,128)(2,1)} copy(bf16[6,16,5120]{2,1,0:T(8,128)(2,1)S(1)} %bitcast.67) | data formatting | bytes 1966080 | tf_op jit(solution)/shard_map/convert_element_type | solution.py:100
  180.4 10.6 %reshape.179 = bf16[16,2,15360]{2,1,0:T(2,128)(2,1)S(1)} reshape(bf16[5120,6,16]{2,1,0:T(8,128)(2,1)} %bitcast.63) | data formatting | bytes 1966080
  191.1 25.5 %all_to_all.33 = bf16[16,2,15360]{2,1,0:T(2,128)(2,1)S(1)} all-to-all(bf16[16,2,15360]{2,1,0:T(2,128)(2,1)S(1)} %reshape.179), channel_id=1, replica_groups=mesh['lat'=8,'ord'=16] {'ord'}, dimensions={0} | all-to-all | bytes 1966080 | tf_op jit(solution)/shard_map/all_to_all | solution.py:103
  216.5 10.8 %reshape.180 = bf16[5120,6,16]{2,1,0:T(8,128)(2,1)} reshape(bf16[16,2,15360]{2,1,0:T(2,128)(2,1)S(1)} %all_to_all.33) | data formatting | bytes 1966080
  227.3 8.6 %copy.92 = bf16[6,16,16,320]{3,2,1,0:T(8,128)(2,1)S(1)} copy(bf16[6,16,16,320]{2,0,3,1:T(8,128)(2,1)} %bitcast.64) | data formatting | bytes 1966080 | tf_op jit(solution)/shard_map/all_to_all | solution.py:103
  236.0 1.2 copy.93
  237.2 0.0 copy-start.3
  237.2 27.0 %fusion.54 = f32[6,320,128]{2,0,1:T(8,128)S(1)} fusion(bf16[6,256,320]{1,0,2:T(8,128)(2,1)S(1)} %copy.93, bf16[256,320,128]{2,1,0:T(8,128)(2,1)} %param.5), kind=kOutput, calls=%fused_computation.63 | convolution fusion | flops 125829120 | bytes 22937600 | tf_op jit(solution)/shard_map/xrk,rkn->xkn/dot_general | solution.py:101
  264.2 1.1 copy.95
  265.4 0.0 all-reduce.2.cloned.1.call-update
  265.5 0.1 compare_convert_fusion
  265.6 69.9 %all-reduce.2.cloned.1.call-done = f32[3,2,320,128]{3,2,1,0:T(8,128)} async-done(((f32[3,2,320,128]{3,2,1,0:T(8,128)}), f32[3,2,320,128]{3,2,1,0:T(8,128)}) %all-reduce.2.cloned.1.call-update) | async-done | bytes 983056 | tf_op jit(solution)/shard_map/psum | solution.py:118
  335.5 1.3 multiply_reduce_fusion
  336.8 28.5 %fusion.61 = f32[2,256,320]{1,0,2:T(2,128)S(1)} fusion(bf16[256,320,128]{2,1,0:T(8,128)(2,1)} %param.5, bf16[2,320,128]{2,1,0:T(8,128)(2,1)S(1)} %multiply_convert_fusion), kind=kOutput, calls=%fused_computation.72 | convolution fusion | flops 41943040 | bytes 21790720 | tf_op jit(solution)/shard_map/rkn,ckn->crk/dot_general | solution.py:121
  365.3 1.3 copy.98
  366.6 12.4 %all-to-all-start.1 = ((f32[2,256,320]{2,0,1:T(2,128)}), f32[2,256,320]{2,0,1:T(2,128)S(1)}, u32[]{:S(2)}, u32[]{:S(2)}) async-start(f32[2,256,320]{2,0,1:T(2,128)} %copy.98), calls=%async_computation.1 | async-start | bytes 1572864 | tf_op jit(solution)/shard_map/all_to_all | solution.py:122
  379.0 26.6 %fusion.31 = (f32[180,29,240]{2,1,0:T(8,128)}, f32[180,29,240]{2,1,0:T(8,128)}, f32[180,29,240]{2,1,0:T(8,128)}) fusion(s32[29,240]{1,0:T(8,128)S(1)} %iota_multiply_fusion.2, s32[180,240]{1,0:T(8,128)S(1)} %iota_multiply_fusion), kind=kLoop, calls=%fused_computation.42 | loop fusion | flops 12528000 | bytes 15234240 | tf_op jit(solution)/shard_map/sin | solution.py:28
  405.6 0.0 all-to-all-done.1
  405.6 0.1 copy.99
  405.7 0.1 fusion.109
  405.7 0.1 copy.100
  405.9 0.1 reshape.152
  406.0 2.2 copy.101
  408.3 14.0 %scatter_custom_fusion = f32[16,5220]{0,1:T(8,128)S(1)} fusion(s32[5120]{0:T(1024)S(1)} %get-tuple-element.20, f32[5120,16]{1,0:T(8,128)} %copy.101, f32[]{:T(128)} %constant.52.clone.1), kind=kCustom, calls=%fused_computation.68 | custom fusion | bytes 334592 | tf_op jit(solution)/shard_map/scatter | solution.py:126
  422.3 0.7 copy.102
  423.0 0.7 reshape.133
  423.7 2.0 copy.103
  425.8 0.1 copy.104
  425.9 0.1 reshape.160
  426.0 2.2 copy.105
  428.3 14.0 %scatter_custom_fusion.1 = f32[16,5220]{0,1:T(8,128)S(1)} fusion(s32[5120]{0:T(1024)S(1)} %get-tuple-element.20, f32[5120,16]{1,0:T(8,128)} %copy.105, f32[]{:T(128)} %constant.52.clone.1), kind=kCustom, calls=%fused_computation.66 | custom fusion | bytes 334592 | tf_op jit(solution)/shard_map/scatter | solution.py:129
  442.3 0.7 copy.106
  443.1 0.7 reshape.134
  443.7 2.0 copy.107
  445.8 23.8 %fusion.39 = f32[16,180,480]{2,0,1:T(8,128)S(1)} fusion(f32[180,29,240]{2,1,0:T(8,128)} %get-tuple-element.18, f32[180,29,240]{2,1,0:T(8,128)} %get-tuple-element.17, f32[180,29,240]{2,1,0:T(8,128)} %get-tuple-element.16, f32[16,180,29]{2,0,1:T(8,128)} %bitcast.74, f32[16,180,29]{2,0,1:T(8,128)} %bitcast.73), kind=kOutput, calls=%fused_computation.56 | convolution fusion | flops 977351040 | bytes 21231360 | tf_op jit(solution)/shard_map/rkq,kqj->rkj/dot_general | solution.py:70
  469.6 1.1 fusion.108
  470.7 4.9 %fusion.35 = f32[180,16,240]{2,0,1:T(8,128)S(1)} fusion(f32[16,180,240]{2,0,1:T(8,128)S(1)} %get-tuple-element.6), kind=kOutput, calls=%fused_computation.49 | convolution fusion | flops 1493283584 | bytes 5529600 | tf_op jit(solution)/shard_map/rkj,ka->raj/dot_general | solution.py:73
  475.6 5.1 %multiply_bitcast_fusion = f32[16,180,240]{2,1,0:T(8,128)S(1)} fusion(f32[180,16,240]{2,0,1:T(8,128)S(1)} %fusion.35, f32[16,180,240]{2,0,1:T(8,128)S(1)} %get-tuple-element.5), kind=kOutput, calls=%fused_computation.53 | convolution fusion | flops 1494665984 | bytes 8294400 | tf_op jit(solution)/shard_map/rkj,ka->raj/dot_general | solution.py:72
  480.7 2.5 mul.334
  (15 shorter events, 0.1 us)
Async XLA Ops:
  6.5 1.8 copy-start.1
  6.5 328.9 %all-reduce.2.cloned.1.call-start = ((), (), s32[]{:S(2)}) async-start(), calls=%async_computation.2 | async-start | bytes 1966080 | tf_op jit(solution)/shard_map/psum | solution.py:118
  23.5 13.3 %copy-start = (f32[48,180,240]{2,1,0:T(8,128)S(1)}, f32[48,180,240]{2,1,0:T(8,128)}, u32[]{:S(2)}) copy-start(f32[48,180,240]{2,1,0:T(8,128)} %reshape.129) | copy-start | bytes 24883204
  128.7 3.8 copy-start.2
  237.2 28.3 %copy-start.3 = (s32[320]{0:T(512)S(1)}, s32[320]{0:T(512)}, u32[]{:S(2)}) copy-start(s32[320]{0:T(512)} %param.7) | copy-start | bytes 3844
  366.6 39.0 %all-to-all-start.1 = ((f32[2,256,320]{2,0,1:T(2,128)}), f32[2,256,320]{2,0,1:T(2,128)S(1)}, u32[]{:S(2)}, u32[]{:S(2)}) async-start(f32[2,256,320]{2,0,1:T(2,128)} %copy.98), calls=%async_computation.1 | async-start | bytes 1572864 | tf_op jit(solution)/shard_map/all_to_all | solution.py:122
Sparse Core Ops, SparseCore 0:
  265.5 69.8 all-reduce.1
where the time goes:
time: 497 us; the launch traced here: 490 us
  matrix products  151 us (30%)
  local copies, waits for them, and re-layouts  145 us (29%)
  other arithmetic  72.2 us (15%)
  waiting for transfers between devices  69.9 us (14%)
  blocking collectives  25.5 us (5%)
  between operations  14 us (3%)
  starting transfers between devices  12.4 us (2%)
    psum x1, waiting for transfers between devices, local(): total = lax.psum(sums, 'lat')  69.9 us
    dot_general x1, matrix products, forward_spectra(): jnp.einsum('rkj,kjq->rkq', joined, table, precision=lax.Precision.HIGHEST)  38.4 us
    scatter x4, local copies, waits for them, and re-layouts, local(): jnp.zeros((cycle_dev, blocks * LON_SLOW), jnp.float32).at[:, target]  29.5 us
    dot_general x1, matrix products, local(): jnp.einsum('rkn,ckn->crk', panels, coeffs, preferred_element_type=jnp.flo...  28.5 us
    dot_general x1, matrix products, local(): jnp.einsum('xrk,rkn->xkn', lax.all_to_all(picked, 'ord', split_axis=2, co...  27 us
    sin x1, other arithmetic, twiddle_tables(): return (jnp.cos(angle), jnp.sin(angle))  26.6 us
    neg x1, other arithmetic, forward_spectra(): -twist_sin  26.4 us
    all_to_all x1, blocking collectives, local(): lax.all_to_all(picked, 'ord', split_axis=2, concat_axis=1, tiled=True)  25.5 us
  transfers between devices with their start and end apart: 2, of which 1 were waited for; matrix products, arithmetic and copies ran while one was open for 5% of the time, Pallas kernels for 0%

commit v1 on v0

--- a/solution.py
+++ b/solution.py
@@ -115,7 +115,8 @@
         ]
     )
     keep = (degree_int[None, :] <= cutoffs[:, None]).astype(jnp.float32)
-    total = lax.psum(sums, "lat")
+    parts = lax.all_gather(sums, "lat")
+    total = jnp.sum(parts, axis=0)
     folded = fold_powers(total, factors)
     coeffs = (folded * keep[None]).astype(jnp.bfloat16)
     synthesis = jnp.einsum("rkn,ckn->crk", panels, coeffs, preferred_element_type=jnp.float32)

time: 497 us -> 584 us (1.18)
  waiting for transfers between devices: 69.9 us -> 156 us
    all_gather x0 -> x1, waiting for transfers between devices: none -> 156 us  [local(): parts = lax.all_gather(sums, 'lat')]
    psum x1 -> x0, waiting for transfers between devices: 69.9 us -> none  [local(): total = lax.psum(sums, 'lat')]
where the time goes in v1:
time: 584 us; the launch traced here: 574 us
  waiting for transfers between devices  156 us (27%)
  matrix products  151 us (26%)
  local copies, waits for them, and re-layouts  145 us (25%)
  other arithmetic  74.7 us (13%)
  blocking collectives  25.5 us (4%)
  between operations  14 us (2%)
  starting transfers between devices  7.31 us (1%)
    all_gather x1, waiting for transfers between devices, local(): parts = lax.all_gather(sums, 'lat')  156 us
    dot_general x1, matrix products, forward_spectra(): jnp.einsum('rkj,kjq->rkq', joined, table, precision=lax.Precision.HIGHEST)  38.4 us
    scatter x4, local copies, waits for them, and re-layouts, local(): jnp.zeros((cycle_dev, blocks * LON_SLOW), jnp.float32).at[:, target]  29.5 us
    dot_general x1, matrix products, local(): jnp.einsum('rkn,ckn->crk', panels, coeffs, preferred_element_type=jnp.flo...  28.5 us
    dot_general x1, matrix products, local(): jnp.einsum('xrk,rkn->xkn', lax.all_to_all(picked, 'ord', split_axis=2, co...  27 us
    sin x1, other arithmetic, twiddle_tables(): return (jnp.cos(angle), jnp.sin(angle))  26.6 us
    neg x1, other arithmetic, forward_spectra(): -twist_sin  26.4 us
    all_to_all x1, blocking collectives, local(): lax.all_to_all(picked, 'ord', split_axis=2, concat_axis=1, tiled=True)  25.5 us
  transfers between devices with their start and end apart: 2, of which 1 were waited for; matrix products, arithmetic and copies ran while one was open for 5% of the time, Pallas kernels for 0%

profile of v1, /device:TPU:1, one launch (start us, length us, event | category | flops | bytes accessed | tf_op | source)
XLA Modules:
  0.0 573.9 jit_solution(36800107845283059)
XLA Ops:
  6.5 0.0 all-gather.3.cloned.1.call-start
  6.5 1.8 convert_multiply_fusion.1
  8.4 0.2 convert_element_type.66
  8.5 3.5 pad_maximum_fusion.1
  12.1 11.4 %reshape.129 = f32[48,180,240]{2,1,0:T(8,128)} reshape(f32[48,43200]{1,0:T(8,128)} %pad_maximum_fusion.1) | data formatting | bytes 16588800 | tf_op jit(solution)/shard_map/reshape | solution.py:33
  23.5 13.3 %convolution_bitcast_fusion = f32[48,180,240]{2,1,0:T(8,128)S(1)} fusion(f32[48,180,240]{2,1,0:T(8,128)} %reshape.129), kind=kOutput, calls=%fused_computation.48 | convolution fusion | flops 4479267840 | bytes 16588800 | tf_op jit(solution)/shard_map/raj,ak->rkj/dot_general | solution.py:35
  36.8 9.9 %negate_bitcast_fusion = f32[48,180,240]{2,1,0:T(8,128)S(1)} fusion(f32[48,180,240]{2,1,0:T(8,128)S(1)} %copy-done), kind=kOutput, calls=%fused_computation.26 | convolution fusion | flops 4481341440 | bytes 16588800 | tf_op jit(solution)/shard_map/raj,ak->rkj/dot_general | solution.py:36
  46.8 7.9 %pad_maximum_fusion = f32[48,180,480]{2,1,0:T(8,128)} fusion(f32[48,180,240]{2,1,0:T(8,128)S(1)} %negate_bitcast_fusion, f32[48,180,240]{2,1,0:T(8,128)S(1)} %convolution_bitcast_fusion), kind=kLoop, calls=%fused_computation.24 | loop fusion | flops 4147200 | bytes 33177600 | tf_op jit(solution)/shard_map/concatenate | solution.py:39
  54.7 26.4 %fusion.50 = (f32[180,240,29]{1,2,0:T(8,128)}, f32[180,240,29]{1,2,0:T(8,128)}, f32[180,240,29]{1,2,0:T(8,128)}) fusion(s32[240,29]{0,1:T(8,128)S(1)} %iota_multiply_fusion.1, s32[180,240]{1,0:T(8,128)S(1)} %iota_multiply_fusion), kind=kLoop, calls=%fused_computation.59 | loop fusion | flops 12528000 | bytes 15234240 | tf_op jit(solution)/shard_map/neg | solution.py:41
  81.1 38.4 %fusion.42 = f32[48,180,58]{2,0,1:T(8,128)S(1)} fusion(f32[48,180,480]{2,1,0:T(8,128)} %pad_maximum_fusion, f32[180,240,29]{1,2,0:T(8,128)} %get-tuple-element.15, f32[180,240,29]{1,2,0:T(8,128)} %get-tuple-element.14, f32[180,240,29]{1,2,0:T(8,128)} %get-tuple-element.13), kind=kOutput, calls=%fused_computation.57 | convolution fusion | flops 2901484800 | bytes 33626880 | tf_op jit(solution)/shard_map/rkj,kjq->rkq/dot_general | solution.py:43
  119.5 4.8 slice_bitcast_fusion.1
  124.3 4.4 copy.136
  128.7 0.0 copy-start.2
  128.7 1.7 reshape.174
  130.4 2.1 slice_multiply_fusion.1
  132.5 15.1 %gather_fusion = bf16[5120,48]{1,0:T(8,128)(2,1)S(1)} fusion(bf16[48,5120]{0,1:T(8,128)(2,1)S(1)} %slice_multiply_fusion.1, s32[5120]{0:T(1024)S(1)} %get-tuple-element.19), kind=kCustom, calls=%fused_computation | custom fusion | bytes 1003520 | tf_op jit(solution)/shard_map/gather | solution.py:95
  147.6 0.6 copy.111
  148.2 4.4 copy.137
  152.6 1.7 reshape.175
  154.3 2.1 slice_multiply_fusion
  156.4 15.1 %gather_fusion.1 = bf16[5120,48]{1,0:T(8,128)(2,1)S(1)} fusion(bf16[48,5120]{0,1:T(8,128)(2,1)S(1)} %slice_multiply_fusion, s32[5120]{0:T(1024)S(1)} %get-tuple-element.19), kind=kCustom, calls=%fused_computation.1 | custom fusion | bytes 1003520 | tf_op jit(solution)/shard_map/gather | solution.py:96
  171.5 0.6 copy.114
  172.1 0.1 pad_maximum_fusion.2
  172.2 0.1 copy.115
  172.3 8.1 %copy.116 = bf16[6,16,5120]{1,0,2:T(8,128)(2,1)} copy(bf16[6,16,5120]{2,1,0:T(8,128)(2,1)S(1)} %bitcast.69) | data formatting | bytes 1966080 | tf_op jit(solution)/shard_map/convert_element_type | solution.py:100
  180.4 10.6 %reshape.180 = bf16[16,2,15360]{2,1,0:T(2,128)(2,1)S(1)} reshape(bf16[5120,6,16]{2,1,0:T(8,128)(2,1)} %bitcast.64) | data formatting | bytes 1966080
  191.1 25.5 %all_to_all.33 = bf16[16,2,15360]{2,1,0:T(2,128)(2,1)S(1)} all-to-all(bf16[16,2,15360]{2,1,0:T(2,128)(2,1)S(1)} %reshape.180), channel_id=1, replica_groups=mesh['lat'=8,'ord'=16] {'ord'}, dimensions={0} | all-to-all | bytes 1966080 | tf_op jit(solution)/shard_map/all_to_all | solution.py:103
  216.5 10.8 %reshape.181 = bf16[5120,6,16]{2,1,0:T(8,128)(2,1)} reshape(bf16[16,2,15360]{2,1,0:T(2,128)(2,1)S(1)} %all_to_all.33) | data formatting | bytes 1966080
  227.3 8.6 %copy.118 = bf16[6,16,16,320]{3,2,1,0:T(8,128)(2,1)S(1)} copy(bf16[6,16,16,320]{2,0,3,1:T(8,128)(2,1)} %bitcast.65) | data formatting | bytes 1966080 | tf_op jit(solution)/shard_map/all_to_all | solution.py:103
  236.0 1.2 copy.119
  237.2 0.0 copy-start.3
  237.2 27.0 %fusion.54 = f32[6,320,128]{2,0,1:T(8,128)S(1)} fusion(bf16[6,256,320]{1,0,2:T(8,128)(2,1)S(1)} %copy.119, bf16[256,320,128]{2,1,0:T(8,128)(2,1)} %param.5), kind=kOutput, calls=%fused_computation.63 | convolution fusion | flops 125829120 | bytes 22937600 | tf_op jit(solution)/shard_map/xrk,rkn->xkn/dot_general | solution.py:101
  264.2 1.1 copy.121
  265.4 0.0 all-gather.3.cloned.1.call-update
  265.5 0.1 compare_convert_fusion
  265.6 156.1 %all-gather.3.cloned.1.call-done = f32[48,320,128]{2,1,0:T(8,128)} async-done(((f32[6,320,128]{2,1,0:T(8,128)}), f32[48,320,128]{2,1,0:T(8,128)}) %all-gather.3.cloned.1.call-update) | async-done | bytes 7864336 | tf_op jit(solution)/shard_map/all_gather | solution.py:118
  421.7 3.7 reduce_sum.18
  425.4 0.1 multiply_reduce_fusion
  425.5 28.5 %fusion.61 = f32[2,256,320]{1,0,2:T(2,128)S(1)} fusion(bf16[256,320,128]{2,1,0:T(8,128)(2,1)} %param.5, bf16[2,320,128]{2,1,0:T(8,128)(2,1)S(1)} %multiply_convert_fusion), kind=kOutput, calls=%fused_computation.72 | convolution fusion | flops 41943040 | bytes 21790720 | tf_op jit(solution)/shard_map/rkn,ckn->crk/dot_general | solution.py:122
  454.0 1.3 copy.124
  455.4 7.3 %all-to-all-start.1 = ((f32[2,256,320]{2,0,1:T(2,128)}), f32[2,256,320]{2,0,1:T(2,128)S(1)}, u32[]{:S(2)}, u32[]{:S(2)}) async-start(f32[2,256,320]{2,0,1:T(2,128)} %copy.124), calls=%async_computation.1 | async-start | bytes 1572864 | tf_op jit(solution)/shard_map/all_to_all | solution.py:123
  462.7 26.6 %fusion.31 = (f32[180,29,240]{2,1,0:T(8,128)}, f32[180,29,240]{2,1,0:T(8,128)}, f32[180,29,240]{2,1,0:T(8,128)}) fusion(s32[29,240]{1,0:T(8,128)S(1)} %iota_multiply_fusion.2, s32[180,240]{1,0:T(8,128)S(1)} %iota_multiply_fusion), kind=kLoop, calls=%fused_computation.42 | loop fusion | flops 12528000 | bytes 15234240 | tf_op jit(solution)/shard_map/sin | solution.py:28
  489.3 0.0 all-to-all-done.1
  489.3 0.1 copy.125
  489.3 0.1 fusion.109
  489.4 0.1 copy.126
  489.5 0.1 reshape.152
  489.7 2.2 copy.127
  491.9 14.0 %scatter_custom_fusion = f32[16,5220]{0,1:T(8,128)S(1)} fusion(s32[5120]{0:T(1024)S(1)} %get-tuple-element.20, f32[5120,16]{1,0:T(8,128)} %copy.127, f32[]{:T(128)} %constant.52.clone.1), kind=kCustom, calls=%fused_computation.68 | custom fusion | bytes 334592 | tf_op jit(solution)/shard_map/scatter | solution.py:127
  506.0 0.7 copy.128
  506.7 0.7 reshape.133
  507.4 2.0 copy.129
  509.4 0.1 copy.130
  509.5 0.1 reshape.160
  509.7 2.2 copy.131
  511.9 14.0 %scatter_custom_fusion.1 = f32[16,5220]{0,1:T(8,128)S(1)} fusion(s32[5120]{0:T(1024)S(1)} %get-tuple-element.20, f32[5120,16]{1,0:T(8,128)} %copy.131, f32[]{:T(128)} %constant.52.clone.1), kind=kCustom, calls=%fused_computation.66 | custom fusion | bytes 334592 | tf_op jit(solution)/shard_map/scatter | solution.py:130
  526.0 0.7 copy.132
  526.7 0.7 reshape.134
  527.4 2.0 copy.133
  529.4 23.8 %fusion.39 = f32[16,180,480]{2,0,1:T(8,128)S(1)} fusion(f32[180,29,240]{2,1,0:T(8,128)} %get-tuple-element.18, f32[180,29,240]{2,1,0:T(8,128)} %get-tuple-element.17, f32[180,29,240]{2,1,0:T(8,128)} %get-tuple-element.16, f32[16,180,29]{2,0,1:T(8,128)} %bitcast.76, f32[16,180,29]{2,0,1:T(8,128)} %bitcast.75), kind=kOutput, calls=%fused_computation.56 | convolution fusion | flops 977351040 | bytes 21231360 | tf_op jit(solution)/shard_map/rkq,kqj->rkj/dot_general | solution.py:70
  553.2 1.1 fusion.108
  554.3 4.9 fusion.35
  559.3 5.1 multiply_bitcast_fusion
  564.4 2.5 mul.334
  (16 shorter events, 0.1 us)
Async XLA Ops:
  6.5 1.8 copy-start.1
  6.5 415.1 %all-gather.3.cloned.1.call-start = ((), (), s32[]{:S(2)}) async-start(), calls=%async_computation.2 | async-start | bytes 8847360 | tf_op jit(solution)/shard_map/all_gather | solution.py:118
  23.5 13.3 %copy-start = (f32[48,180,240]{2,1,0:T(8,128)S(1)}, f32[48,180,240]{2,1,0:T(8,128)}, u32[]{:S(2)}) copy-start(f32[48,180,240]{2,1,0:T(8,128)} %reshape.129) | copy-start | bytes 24883204
  128.7 3.8 copy-start.2
  237.2 28.3 %copy-start.3 = (s32[320]{0:T(512)S(1)}, s32[320]{0:T(512)}, u32[]{:S(2)}) copy-start(s32[320]{0:T(512)} %param.7) | copy-start | bytes 3844
  455.4 33.9 %all-to-all-start.1 = ((f32[2,256,320]{2,0,1:T(2,128)}), f32[2,256,320]{2,0,1:T(2,128)S(1)}, u32[]{:S(2)}, u32[]{:S(2)}) async-start(f32[2,256,320]{2,0,1:T(2,128)} %copy.124), calls=%async_computation.1 | async-start | bytes 1572864 | tf_op jit(solution)/shard_map/all_to_all | solution.py:123
Sparse Core Ops, SparseCore 0:
  265.5 156.1 all-gather.2
